TPU v7x, 32 devices: a whole 2x2x4 slice. The times are simulated.
32 devices in a mesh: group: 2 (over y), ens: 4 (over z), row: 2 (over x), col: 2 (over core).
Axes of the slice: x: 2, y: 2, z: 4, core: 2. Of those that a mesh axis runs over, the one named last changes fastest.
Arguments:
- fields: bfloat16 [4, 128, 256, 128], P('ens', ('group', 'row'), 'col'), parts along dimension 1, may hold values from -6 to 6
- conv_weight: bfloat16 [7, 7, 128], replicated, may hold values from -0.875 to 0.875
- conv_gain: bfloat16 [128], replicated, may hold values from 0.099609375 to 1.8984375
- mlp_in: bfloat16 [128, 512], replicated, may hold values from -0.5 to 0.5
- mlp_out: bfloat16 [512, 128], replicated, may hold values from -0.25 to 0.25
- layer_scale: bfloat16 [128], replicated, may hold values from 0.099609375 to 1.8984375
- attn_gain: bfloat16 [128], replicated, may hold values from 0.099609375 to 1.8984375
- qkv_weight: bfloat16 [3, 128, 128], replicated, may hold values from -1 to 1
- out_weight: bfloat16 [128, 128], replicated, may hold values from -0.5 to 0.5
Outputs:
- result: bfloat16 [4, 128, 256, 128], P('ens', ('group', 'row'), 'col'), parts along dimension 1
There are 2 independent parts, one for each index of `group`. A program takes and returns all parts, laid end to end along the dimension named above; an argument that names none is the same for every part. Nothing has to cross between parts.
All inputs are finite; a program needn't handle non-finite values.
Results may differ from a plain program's by a relative error of at most 0.0065.
Values may be sent and summed in bfloat16 or wider, within the bound.
A program may use at most 64 MiB of HBM per device.

v0:
```python
import jax
import jax.numpy as jnp
from jax import lax
from jax.sharding import PartitionSpec as P

HEADS = 4
KERNEL = 7


def extended(array, sides, width):
    for axis, dim in sides:
        devices, length = (lax.axis_size(axis), array.shape[dim])
        up = [(i, (i + 1) % devices) for i in range(devices - 1)]
        down = [(j, i) for i, j in up]
        last = lax.slice_in_dim(array, length - width, length, axis=dim)
        first = lax.slice_in_dim(array, 0, width, axis=dim)
        before = lax.ppermute(last, axis, up)
        after = lax.ppermute(first, axis, down)
        array = jnp.concatenate([before, array, after], axis=dim)
    return array


def layer_norm(values, gain_vec):
    center = values - jnp.mean(values, axis=-1, keepdims=True)
    spread = jnp.mean(center * center, axis=-1, keepdims=True)
    return center * lax.rsqrt(spread + 1e-06) * gain_vec.astype(jnp.float32)


def mix_members(flat_rows, attn_gain, qkv_weight):
    count, pixels, width = flat_rows.shape
    head_dim = width // HEADS
    normed = layer_norm(flat_rows.astype(jnp.float32), attn_gain).astype(jnp.bfloat16)
    project = jnp.einsum(
        "mpc,jcd->jmpd", normed, qkv_weight, preferred_element_type=jnp.float32
    ).astype(jnp.bfloat16)
    split = project.reshape(3, count, pixels, HEADS, head_dim)
    scores = jnp.einsum(
        "mphd,nphd->hmnp", split[0], split[1], preferred_element_type=jnp.float32
    ) * head_dim ** (-0.5)
    top = jnp.max(scores, axis=2, keepdims=True)
    expo = jnp.exp(scores - top)
    weights = (expo / jnp.sum(expo, axis=2, keepdims=True)).astype(jnp.bfloat16)
    mixed = jnp.einsum(
        "hmnp,nphd->mphd", weights, split[2], preferred_element_type=jnp.float32
    ).astype(jnp.bfloat16)
    return mixed.reshape(count, pixels, width)


def shards(
    fields, conv_weight, conv_gain, mlp_in, mlp_out, layer_scale, attn_gain, qkv_weight, out_weight
):
    members, rows, cols, width = fields.shape
    padded = extended(fields, (("row", 1), ("col", 2)), 3)
    taps = conv_weight.astype(jnp.float32)
    total = jnp.zeros((members, rows, cols, width), jnp.float32)
    for row_tap in range(KERNEL):
        band = padded[:, row_tap : row_tap + rows, :, :]
        partial_row = band[:, :, 0:cols, :].astype(jnp.float32) * taps[row_tap, 0]
        for col_tap in range(1, KERNEL):
            partial_row = (
                partial_row
                + band[:, :, col_tap : col_tap + cols, :].astype(jnp.float32)
                * taps[row_tap, col_tap]
            )
        total = total + partial_row
    normed = layer_norm(total, conv_gain).astype(jnp.bfloat16).reshape(members * rows * cols, width)
    inner = jax.nn.gelu(
        jnp.dot(normed, mlp_in, preferred_element_type=jnp.float32), approximate=True
    ).astype(jnp.bfloat16)
    branch = jnp.dot(inner, mlp_out, preferred_element_type=jnp.float32).reshape(
        members, rows, cols, width
    )
    middle = (fields.astype(jnp.float32) + layer_scale.astype(jnp.float32) * branch).astype(
        jnp.bfloat16
    )
    block = lax.all_to_all(middle, "ens", split_axis=1, concat_axis=0, tiled=True)
    count, block_rows, block_cols, block_width = block.shape
    flat_rows = block.reshape(count, block_rows * block_cols, block_width)
    mixed = mix_members(flat_rows, attn_gain, qkv_weight)
    projected = jnp.einsum("mpc,cd->mpd", mixed, out_weight, preferred_element_type=jnp.float32)
    outcome = (flat_rows.astype(jnp.float32) + projected).astype(jnp.bfloat16)
    outcome = outcome.reshape(count, block_rows, block_cols, block_width)
    gathered = outcome
    gathered = lax.all_to_all(gathered, "ens", split_axis=0, concat_axis=1, tiled=True)
    return gathered


def solution(mesh):
    return jax.shard_map(
        shards,
        mesh=mesh,
        in_specs=(P("ens", ("group", "row"), "col", None), P(), P(), P(), P(), P(), P(), P(), P()),
        out_specs=P("ens", ("group", "row"), "col", None),
        check_vma=False,
    )
```

profile of v0, /device:TPU:0, one launch (start us, length us, event | category | flops | bytes accessed | tf_op | source)
XLA Modules:
  0.0 169.5 jit_solution(12458972681998692937)
XLA Ops:
  0.0 0.0 copy-start
  0.0 0.0 copy-start.1
  0.0 1.0 fusion.44
  1.1 4.8 %collective-permute-start = (bf16[1,3,128,128]{3,2,0,1:T(8,128)(2,1)S(1)}, bf16[1,3,128,128]{3,2,0,1:T(8,128)(2,1)S(1)}, u32[]{:S(2)}, u32[]{:S(2)}) collective-permute-start(bf16[1,3,128,128]{3,2,0,1:T(8,128)(2,1)S(1)} %get-tuple-element.14), channel_id=1, source_target_pairs={{0,2},{1,3},{4,6},{5,7},{8,10},{9,11},{12,14},{13,15},{16,18},{17,... | collective-permute-start | bytes 294920 | tf_op jit(solution)/shard_map/ppermute | solution.py:17
  5.9 1.3 collective-permute-start.1
  7.2 0.7 convert_element_type.209
  8.0 0.1 collective-permute-done
  8.1 4.3 %collective-permute-done.1 = bf16[1,3,128,128]{3,2,0,1:T(8,128)(2,1)S(1)} collective-permute-done((bf16[1,3,128,128]{3,2,0,1:T(8,128)(2,1)S(1)}, bf16[1,3,128,128]{3,2,0,1:T(8,128)(2,1)S(1)}, u32[]{:S(2)}, u32[]{:S(2)}) %collective-permute-start.1) | collective-permute-done | bytes 98336 | tf_op jit(solution)/shard_map/ppermute | solution.py:18
  12.4 0.9 pad_maximum_fusion.5
  13.3 1.3 collective-permute-start.2
  14.6 1.3 collective-permute-start.3
  16.0 0.7 convert_element_type.257
  16.6 0.7 convert_element_type.207
  17.3 0.0 collective-permute-done.2
  17.3 0.5 collective-permute-done.3
  17.7 0.0 copy-done.1
  17.7 1.8 %maximum_maximum_fusion = (bf16[1,38,131,128]{3,2,0,1:T(8,128)(2,1)S(1)}, bf16[1,38,131,128]{3,2,0,1:T(8,128)(2,1)S(1)}) fusion(bf16[1,3,128,128]{3,2,0,1:T(8,128)(2,1)S(1)} %collective-permute-done.1, bf16[1,32,128,128]{3,2,0,1:T(8,128)(2,1)S(1)} %bitcast.150, bf16[1,3,128,128]{3,2,0,1:T(8,128)(2,1)S(1)} %collective-permute-done, ...), kind=kLoop, calls=%fused_computation.34 | loop fusion | flops 10194944 | bytes 3852288 | tf_op jit(solution)/shard_map/concatenate | solution.py:19
  19.5 18.9 %fusion.41 = (f32[32,128]{1,0:T(8,128)S(1)}, f32[1,32,128,128]{3,2,0,1:T(8,128)S(1)}) fusion(f32[128]{0:T(128)S(1)} %get-tuple-element.17, bf16[1,38,131,128]{3,2,0,1:T(8,128)(2,1)S(1)} %get-tuple-element.11, f32[128]{0:T(128)S(1)} %get-tuple-element.18, f32[128]{0:T(128)S(1)} %get-tuple-element.19, f32[128]{0:T(128)S(1)} %get-tuple-element.20, ...), kind=kLoop, calls=%fused_computation.121 | loop fusion | flops 80211968 | bytes 47424000 | tf_op jit(solution)/shard_map/reduce_sum | solution.py:24
  38.5 1.3 multiply_reduce_fusion.1
  39.8 0.0 copy-start.5
  39.8 1.2 multiply_convert_fusion.1
  41.1 0.0 copy-done
  41.1 0.0 copy-done.5
  41.1 0.0 copy-start.2
  41.1 4.4 %fusion.19 = f32[4096,128]{1,0:T(8,128)} fusion(bf16[512,128]{1,0:T(8,128)(2,1)S(1)} %copy-done, bf16[4096,128]{1,0:T(8,128)(2,1)S(1)} %bitcast.159, bf16[128,512]{1,0:T(8,128)(2,1)S(1)} %copy-done.5), kind=kOutput, calls=%fused_computation.29 | convolution fusion | flops 1092616192 | bytes 3407872 | tf_op jit(solution)/shard_map/dot_general | solution.py:70
  45.5 0.0 copy-done.2
  45.5 2.9 %fusion.18 = bf16[1,32,128,128]{3,2,0,1:T(8,128)(2,1)} fusion(f32[1,32,128,128]{3,2,0,1:T(8,128)} %bitcast.158, f32[128]{0:T(128)S(1)} %convert_element_type.207, bf16[1,32,128,128]{3,2,1,0:T(8,128)(2,1)S(1)} %copy-done.2), kind=kLoop, calls=%fused_computation.23 | loop fusion | flops 2097152 | bytes 4194816 | tf_op jit(solution)/shard_map/convert_element_type | solution.py:73
  48.4 0.0 copy-start.6
  48.4 0.0 copy-start.3
  48.4 5.0 %all-to-all-start = ((bf16[1,32,128,128]{3,2,0,1:T(8,128)(2,1)}), bf16[1,32,128,128]{3,2,0,1:T(8,128)(2,1)S(1)}, u32[]{:S(2)}, u32[]{:S(2)}) async-start(bf16[1,32,128,128]{3,2,0,1:T(8,128)(2,1)} %fusion.18), calls=%async_computation | async-start | bytes 2097152 | tf_op jit(solution)/shard_map/all_to_all | solution.py:76
  53.4 0.0 copy-done.6
  53.4 26.6 %all-to-all-done = bf16[1,32,128,128]{3,2,0,1:T(8,128)(2,1)S(1)} async-done(((bf16[1,32,128,128]{3,2,0,1:T(8,128)(2,1)}), bf16[1,32,128,128]{3,2,0,1:T(8,128)(2,1)S(1)}, u32[]{:S(2)}, u32[]{:S(2)}) %all-to-all-start) | async-done | bytes 1048608 | tf_op jit(solution)/shard_map/all_to_all | solution.py:76
  80.0 0.3 convert_reduce_fusion
  80.4 1.3 multiply_reduce_fusion
  81.8 0.0 copy-done.3
  81.8 2.1 %convert_bitcast_fusion = bf16[3,4,1024,128]{2,3,0,1:T(8,128)(2,1)S(1)} fusion(f32[128]{0:T(128)S(1)} %convert_element_type.264, f32[4,1024]{1,0:T(4,128)S(1)} %rsqrt.21, f32[4,1024]{1,0:T(4,128)S(1)} %div.25, bf16[3,128,128]{2,1,0:T(8,128)(2,1)S(1)} %copy-done.3, bf16[4,1024,128]{2,1,0:T(8,128)(2,1)S(1)} %bitcast.146), kind=kOutput, calls=%fused_computation.12 | convolution fusion | flops 406847488 | bytes 4325888 | tf_op jit(solution)/shard_map/mpc,jcd->jmpd/dot_general | solution.py:33
  83.8 1.7 fusion.43
  85.5 6.8 %copy.44 = bf16[4,1024,4,32]{3,0,1,2:T(4,128)(2,1)} copy(bf16[4,1024,4,32]{1,3,2,0:T(8,128)(2,1)} %bitcast.156) | data formatting | bytes 2097152 | tf_op jit(solution)/shard_map/squeeze | solution.py:38
  92.3 6.8 %copy.45 = bf16[4,1024,4,32]{3,0,1,2:T(4,128)(2,1)} copy(bf16[4,1024,4,32]{1,3,2,0:T(8,128)(2,1)} %bitcast.155) | data formatting | bytes 2097152 | tf_op jit(solution)/shard_map/squeeze | solution.py:38
  99.1 8.8 %fusion.47 = f32[4,1024,4,4]{3,2,1,0:T(4,128)} fusion(bf16[4,1024,4,32]{3,0,1,2:T(4,128)(2,1)} %copy.44, bf16[4,1024,4,32]{3,0,1,2:T(4,128)(2,1)} %copy.45), kind=kOutput, calls=%fused_computation.126 | convolution fusion | flops 4194304 | bytes 2359296 | tf_op jit(solution)/shard_map/mphd,nphd->hmnp/dot_general | solution.py:37
  107.9 6.8 %copy.46 = f32[4,1024,4,4]{1,2,3,0:T(4,128)S(1)} copy(f32[4,1024,4,4]{3,2,1,0:T(4,128)} %fusion.47) | data formatting | bytes 524288 | tf_op jit(solution)/shard_map/mphd,nphd->hmnp/dot_general | solution.py:37
  114.7 0.4 fusion.45
  115.1 0.1 divide_convert_fusion
  115.2 5.5 %copy.48 = bf16[4,4,4,1024]{2,1,0,3:T(4,128)(2,1)} copy(bf16[4,4,4,1024]{3,2,1,0:T(4,128)(2,1)S(1)} %divide_convert_fusion) | data formatting | bytes 262144 | tf_op jit(solution)/shard_map/convert_element_type | solution.py:42
  120.6 5.3 %copy.47 = bf16[4,1024,4,32]{3,0,2,1:T(4,128)(2,1)} copy(bf16[4,1024,4,32]{1,3,2,0:T(8,128)(2,1)S(1)} %bitcast.154) | data formatting | bytes 2097152 | tf_op jit(solution)/shard_map/squeeze | solution.py:44
  126.0 8.3 %fusion.9 = bf16[4,1024,4,32]{3,0,2,1:T(4,128)(2,1)} fusion(bf16[4,1024,4,32]{3,0,2,1:T(4,128)(2,1)} %copy.47, bf16[4,4,4,1024]{2,1,0,3:T(4,128)(2,1)} %copy.48), kind=kOutput, calls=%fused_computation.11 | convolution fusion | flops 4718592 | bytes 2228224 | tf_op jit(solution)/shard_map/hmnp,nphd->mphd/dot_general | solution.py:43
  134.3 0.0 copy-start.4
  134.3 5.5 %copy.49 = bf16[4,1024,4,32]{1,3,2,0:T(8,128)(2,1)S(1)} copy(bf16[4,1024,4,32]{3,0,2,1:T(4,128)(2,1)} %fusion.9) | data formatting | bytes 2097152 | tf_op jit(solution)/shard_map/convert_element_type | solution.py:45
  139.9 0.0 copy-done.4
  139.9 0.5 add_convert_fusion
  140.3 28.2 %all_to_all.21 = bf16[4,8,128,128]{3,2,1,0:T(8,128)(2,1)S(1)} all-to-all(bf16[4,8,128,128]{3,2,1,0:T(8,128)(2,1)S(1)} %bitcast.153), channel_id=1, replica_groups=mesh['group'=2,'ens'=4,'row'=2,'col'=2] {'ens'}, dimensions={0} | all-to-all | bytes 2097152 | tf_op jit(solution)/shard_map/all_to_all | solution.py:84
  168.6 1.0 copy.56
  (10 shorter events, 0.1 us)
Async XLA Ops:
  0.0 41.1 %copy-start = (bf16[512,128]{1,0:T(8,128)(2,1)S(1)}, bf16[512,128]{1,0:T(8,128)(2,1)}, u32[]{:S(2)}) copy-start(bf16[512,128]{1,0:T(8,128)(2,1)} %param.13) | copy-start | bytes 393220
  0.0 17.7 %copy-start.1 = (bf16[1,32,128,128]{3,2,1,0:T(8,128)(2,1)S(1)}, bf16[1,32,128,128]{3,2,1,0:T(8,128)(2,1)}, u32[]{:S(2)}) copy-start(bf16[1,32,128,128]{3,2,1,0:T(8,128)(2,1)} %param.9) | copy-start | bytes 3145732
  1.1 7.0 %collective-permute-start = (bf16[1,3,128,128]{3,2,0,1:T(8,128)(2,1)S(1)}, bf16[1,3,128,128]{3,2,0,1:T(8,128)(2,1)S(1)}, u32[]{:S(2)}, u32[]{:S(2)}) collective-permute-start(bf16[1,3,128,128]{3,2,0,1:T(8,128)(2,1)S(1)} %get-tuple-element.14), channel_id=1, source_target_pairs={{0,2},{1,3},{4,6},{5,7},{8,10},{9,11},{12,14},{13,15},{16,18},{17,... | collective-permute-start | bytes 294920 | tf_op jit(solution)/shard_map/ppermute | solution.py:17
  5.9 6.5 %collective-permute-start.1 = (bf16[1,3,128,128]{3,2,0,1:T(8,128)(2,1)S(1)}, bf16[1,3,128,128]{3,2,0,1:T(8,128)(2,1)S(1)}, u32[]{:S(2)}, u32[]{:S(2)}) collective-permute-start(bf16[1,3,128,128]{3,2,0,1:T(8,128)(2,1)S(1)} %get-tuple-element.15), channel_id=1, source_target_pairs={{2,0},{3,1},{6,4},{7,5},{10,8},{11,9},{14,12},{15,13},{18,16},{19,... | collective-permute-start | bytes 294920 | tf_op jit(solution)/shard_map/ppermute | solution.py:18
  13.3 3.9 %collective-permute-start.2 = (bf16[1,38,3,128]{3,2,0,1:T(4,128)(2,1)S(1)}, bf16[1,38,3,128]{3,2,0,1:T(4,128)(2,1)S(1)}, u32[]{:S(2)}, u32[]{:S(2)}) collective-permute-start(bf16[1,38,3,128]{3,2,0,1:T(4,128)(2,1)S(1)} %get-tuple-element.12), channel_id=1, source_target_pairs={{0,1},{2,3},{4,5},{6,7},{8,9},{10,11},{12,13},{14,15},{16,17},{18,... | collective-permute-start | bytes 87560 | tf_op jit(solution)/shard_map/ppermute | solution.py:17
  14.6 3.1 %collective-permute-start.3 = (bf16[1,38,3,128]{3,2,0,1:T(4,128)(2,1)S(1)}, bf16[1,38,3,128]{3,2,0,1:T(4,128)(2,1)S(1)}, u32[]{:S(2)}, u32[]{:S(2)}) collective-permute-start(bf16[1,38,3,128]{3,2,0,1:T(4,128)(2,1)S(1)} %get-tuple-element.13), channel_id=1, source_target_pairs={{1,0},{3,2},{5,4},{7,6},{9,8},{11,10},{13,12},{15,14},{17,16},{19,... | collective-permute-start | bytes 87560 | tf_op jit(solution)/shard_map/ppermute | solution.py:18
  39.8 1.3 copy-start.5
  41.1 4.5 %copy-start.2 = (bf16[1,32,128,128]{3,2,1,0:T(8,128)(2,1)S(1)}, bf16[1,32,128,128]{3,2,1,0:T(8,128)(2,1)}, u32[]{:S(2)}) copy-start(bf16[1,32,128,128]{3,2,1,0:T(8,128)(2,1)} %param.9) | copy-start | bytes 3145732
  48.4 5.0 %copy-start.6 = (bf16[128]{0:T(256)(128)(2,1)S(1)}, bf16[128]{0:T(256)(128)(2,1)}, u32[]{:S(2)}) copy-start(bf16[128]{0:T(256)(128)(2,1)} %param.15) | copy-start | bytes 772
  48.4 33.3 %copy-start.3 = (bf16[3,128,128]{2,1,0:T(8,128)(2,1)S(1)}, bf16[3,128,128]{2,1,0:T(8,128)(2,1)}, u32[]{:S(2)}) copy-start(bf16[3,128,128]{2,1,0:T(8,128)(2,1)} %param.16) | copy-start | bytes 294916
  48.4 31.6 %all-to-all-start = ((bf16[1,32,128,128]{3,2,0,1:T(8,128)(2,1)}), bf16[1,32,128,128]{3,2,0,1:T(8,128)(2,1)S(1)}, u32[]{:S(2)}, u32[]{:S(2)}) async-start(bf16[1,32,128,128]{3,2,0,1:T(8,128)(2,1)} %fusion.18), calls=%async_computation | async-start | bytes 2097152 | tf_op jit(solution)/shard_map/all_to_all | solution.py:76
  134.3 5.5 %copy-start.4 = (bf16[128,128]{1,0:T(8,128)(2,1)S(1)}, bf16[128,128]{1,0:T(8,128)(2,1)}, u32[]{:S(2)}) copy-start(bf16[128,128]{1,0:T(8,128)(2,1)} %param.17) | copy-start | bytes 98308
where the time goes:
time: 171 us; the launch traced here: 170 us
  local copies, waits for them, and re-layouts  40.5 us (24%)
  waiting for transfers between devices  31.5 us (18%)
  other arithmetic  31.2 us (18%)
  blocking collectives  28.2 us (16%)
  matrix products  24.2 us (14%)
  starting transfers between devices  13.7 us (8%)
    all_to_all x1, blocking collectives, shards(): lax.all_to_all(gathered, 'ens', split_axis=0, concat_axis=1, tiled=True)  28.2 us
    all_to_all x1, waiting for transfers between devices, shards(): lax.all_to_all(middle, 'ens', split_axis=1, concat_axis=0, tiled=True)  26.6 us
    reduce_sum x2, other arithmetic, layer_norm(): center = values - jnp.mean(values, axis=-1, keepdims=True)  19.3 us
    dot_general x1, matrix products, mix_members(): jnp.einsum('mphd,nphd->hmnp', split[0], split[1], preferred_element_type=...  8.83 us
    dot_general x1, matrix products, mix_members(): jnp.einsum('hmnp,nphd->mphd', weights, split[2], preferred_element_type=j...  8.34 us
    dot_general x1, local copies, waits for them, and re-layouts, mix_members(): jnp.einsum('mphd,nphd->hmnp', split[0], split[1], preferred_element_type=...  6.82 us
    squeeze x1, local copies, waits for them, and re-layouts, mix_members(): split[1]  6.79 us
    squeeze x1, local copies, waits for them, and re-layouts, mix_members(): split[0]  6.77 us
  transfers between devices with their start and end apart: 5, of which 4 were waited for; matrix products, arithmetic and copies ran while one was open for 1% of the time, Pallas kernels for 0%

commit v1 on v0

--- a/solution.py
+++ b/solution.py
@@ -73,7 +73,18 @@
     middle = (fields.astype(jnp.float32) + layer_scale.astype(jnp.float32) * branch).astype(
         jnp.bfloat16
     )
-    block = lax.all_to_all(middle, "ens", split_axis=1, concat_axis=0, tiled=True)
+    ways, here = (lax.axis_size("ens"), lax.axis_index("ens"))
+    width_2 = middle.shape[1] // ways
+    shape = list(middle.shape)
+    shape[1] = width_2
+    height = shape[0]
+    shape[0] = height * ways
+    block = jnp.zeros(shape, middle.dtype)
+    for mask in range(ways):
+        part = lax.dynamic_slice_in_dim(middle, (here ^ mask) * width_2, width_2, axis=1)
+        if mask:
+            part = lax.ppermute(part, "ens", [(d, d ^ mask) for d in range(ways)])
+        block = lax.dynamic_update_slice_in_dim(block, part, (here ^ mask) * height, axis=0)
     count, block_rows, block_cols, block_width = block.shape
     flat_rows = block.reshape(count, block_rows * block_cols, block_width)
     mixed = mix_members(flat_rows, attn_gain, qkv_weight)

time: 171 us -> 186 us (1.088)
  other arithmetic: 31.2 us -> 51 us
  waiting for transfers between devices: 31.5 us -> 18.9 us
  blocking collectives: 28.2 us -> 33.9 us
  local copies, waits for them, and re-layouts: 40.5 us -> 44.4 us
    all_to_all x1 -> x0, waiting for transfers between devices: 26.6 us -> none  [shards(): lax.all_to_all(middle, 'ens', split_axis=1, concat_axis=0, tiled=True)]
    reduce_sum x2, other arithmetic: 19.3 us -> 41.3 us  [layer_norm(): center = values - jnp.mean(values, axis=-1, keepdims=True)]
    ppermute x0 -> x3, waiting for transfers between devices: none -> 18.7 us  [shards(): part = lax.ppermute(part, 'ens', [(d, d ^ mask) for d in range(ways)])]
    all_to_all x1, blocking collectives: 28.2 us -> 33.9 us  [shards(): lax.all_to_all(gathered, 'ens', split_axis=0, concat_axis=1, tiled=True)]
    ppermute x0 -> x3, starting transfers between devices: none -> 5.32 us  [shards(): part = lax.ppermute(part, 'ens', [(d, d ^ mask) for d in range(ways)])]
    all_to_all x1 -> x0, starting transfers between devices: 5.01 us -> none  [shards(): lax.all_to_all(middle, 'ens', split_axis=1, concat_axis=0, tiled=True)]
    ppermute x2, waiting for transfers between devices: 4.79 us -> 0.01 us  [extended(): after = lax.ppermute(first, axis, down)]
    convert_element_type x1, other arithmetic: 2.88 us -> 0.33 us  [shards(): (fields.astype(jnp.float32) + layer_scale.astype(jnp.float32) * branch).a...]
  transfers between devices with their start and end apart: 5 -> 7, of which waited for: 4 -> 3; matrix products, arithmetic and copies ran while one was open for 1% -> 4% of each run, Pallas kernels for 0% -> 0%
where the time goes in v1:
time: 186 us
  other arithmetic  51 us (27%)
  local copies, waits for them, and re-layouts  44.4 us (24%)
  blocking collectives  33.9 us (18%)
  matrix products  23 us (12%)
  waiting for transfers between devices  18.9 us (10%)
  starting transfers between devices  14.1 us (8%)
    reduce_sum x2, other arithmetic, layer_norm(): center = values - jnp.mean(values, axis=-1, keepdims=True)  41.3 us
    all_to_all x1, blocking collectives, shards(): lax.all_to_all(gathered, 'ens', split_axis=0, concat_axis=1, tiled=True)  33.9 us
    ppermute x3, waiting for transfers between devices, shards(): part = lax.ppermute(part, 'ens', [(d, d ^ mask) for d in range(ways)])  18.7 us
    dot_general x1, matrix products, mix_members(): jnp.einsum('mphd,nphd->hmnp', split[0], split[1], preferred_element_type=...  8.83 us
    dot_general x1, matrix products, mix_members(): jnp.einsum('hmnp,nphd->mphd', weights, split[2], preferred_element_type=j...  8.35 us
    dot_general x1, local copies, waits for them, and re-layouts, mix_members(): jnp.einsum('mphd,nphd->hmnp', split[0], split[1], preferred_element_type=...  6.82 us
    squeeze x1, local copies, waits for them, and re-layouts, mix_members(): split[1]  6.77 us
    ppermute x2, starting transfers between devices, extended(): before = lax.ppermute(last, axis, up)  6.2 us
  transfers between devices with their start and end apart: 7, of which 3 were waited for; matrix products, arithmetic and copies ran while one was open for 4% of the time, Pallas kernels for 0%

profile of v1, /device:TPU:0, one launch (start us, length us, event | category | flops | bytes accessed | tf_op | source)
XLA Modules:
  0.0 185.7 jit_solution(18038141689109426230)
XLA Ops:
  0.0 0.0 copy-start
  0.0 1.0 fusion.84
  1.0 1.3 collective-permute-start.1
  2.3 4.9 %collective-permute-start = (bf16[1,3,128,128]{3,2,1,0:T(8,128)(2,1)S(1)}, bf16[1,3,128,128]{3,2,1,0:T(8,128)(2,1)S(1)}, u32[]{:S(2)}, u32[]{:S(2)}) collective-permute-start(bf16[1,3,128,128]{3,2,1,0:T(8,128)(2,1)S(1)} %get-tuple-element.20), channel_id=1, source_target_pairs={{0,2},{1,3},{4,6},{5,7},{8,10},{9,11},{12,14},{13,15},{16,18},{17,... | collective-permute-start | bytes 294920 | tf_op jit(solution)/shard_map/ppermute | solution.py:17
  7.2 0.7 convert_element_type.204
  7.9 0.6 slice_bitcast_fusion.47
  8.5 0.7 slice_bitcast_fusion.48
  9.2 0.1 collective-permute-done
  9.4 0.0 copy-start.1
  9.4 2.2 %constant_dynamic-update-slice_fusion.3 = (bf16[1,35,128,128]{3,2,1,0:T(8,128)(2,1)S(1)}, bf16[1,38,128,128]{3,2,1,0:T(8,128)(2,1)S(1)}, bf16[1,35,128,128]{3,2,1,0:T(8,128)(2,1)S(1)}) fusion(bf16[1,35,128,128]{3,2,1,0:T(8,128)(2,1)S(1)} %get-tuple-element.21, bf16[1,32,128,128]{3,2,1,0:T(8,128)(2,1)} %param.9, ...), kind=kLoop, calls=%fused_computation.150 | loop fusion | bytes 4194304 | tf_op jit(solution)/shard_map/concatenate | solution.py:19
  11.6 0.0 collective-permute-done.1
  11.7 0.0 copy-start.2
  11.7 1.0 copy-done.2
  12.7 0.7 fusion.83
  13.4 1.3 collective-permute-start.2
  14.8 1.3 collective-permute-start.3
  16.1 0.6 slice_bitcast_fusion.46
  16.7 1.1 convert_element_type.252
  17.8 1.2 convert_element_type.202
  19.0 0.0 collective-permute-done.2
  19.0 0.0 collective-permute-done.3
  19.0 0.0 copy-done.1
  19.0 40.9 %fusion.80 = (f32[32,128]{1,0:T(8,128)S(1)}, f32[1,32,128,128]{3,2,1,0:T(8,128)S(1)}) fusion(f32[128]{0:T(128)} %get-tuple-element.26, bf16[1,38,3,128]{3,2,1,0:T(4,128)(2,1)S(1)} %collective-permute-done.3, bf16[1,38,128,128]{3,2,1,0:T(8,128)(2,1)} %copy-done.2, f32[128]{0:T(128)} %get-tuple-element.27, f32[128]{0:T(128)} %get-tuple-element.28, ...), kind=kLoop, calls=%fused_computation.219 | loop fusion | flops 143126528 | bytes 10782208 | tf_op jit(solution)/shard_map/reduce_sum | solution.py:24
  60.0 0.0 copy-start.6
  60.0 1.3 multiply_reduce_fusion
  61.3 0.0 copy-start.7
  61.3 0.0 copy-done.6
  61.4 2.0 %multiply_convert_fusion = bf16[1,32,128,128]{3,2,1,0:T(8,128)(2,1)} fusion(f32[1,32,128,128]{3,2,1,0:T(8,128)S(1)} %get-tuple-element.6, f32[128]{0:T(128)S(1)} %copy-done.6, f32[32,128]{1,0:T(8,128)S(1)} %add_rsqrt_fusion, f32[32,128]{1,0:T(8,128)S(1)} %broadcast_multiply_fusion.1), kind=kLoop, calls=%fused_computation.74 | loop fusion | flops 2097152 | bytes 3179008 | tf_op jit(solution)/shard_map/convert_element_type | solution.py:66
  63.4 0.0 copy-done
  63.4 0.0 copy-done.7
  63.4 4.3 %fusion.25 = f32[4096,128]{1,0:T(8,128)S(1)} fusion(bf16[512,128]{1,0:T(8,128)(2,1)S(1)} %copy-done, bf16[4096,128]{1,0:T(8,128)(2,1)} %bitcast.161, bf16[128,512]{1,0:T(8,128)(2,1)S(1)} %copy-done.7), kind=kOutput, calls=%fused_computation.76 | convolution fusion | flops 1092616192 | bytes 3407872 | tf_op jit(solution)/shard_map/dot_general | solution.py:70
  67.7 0.0 copy-done.5
  67.8 0.3 fusion.18
  68.1 0.0 copy-start.8
  68.1 0.2 broadcast_in_dim.2
  68.3 0.1 constant_dynamic-slice_fusion
  68.4 2.7 %collective-permute-start.4 = (bf16[1,8,128,128]{3,2,1,0:T(8,128)(2,1)S(1)}, bf16[1,8,128,128]{3,2,1,0:T(8,128)(2,1)S(1)}, u32[]{:S(2)}, u32[]{:S(2)}) collective-permute-start(bf16[1,8,128,128]{3,2,1,0:T(8,128)(2,1)S(1)} %get-tuple-element.14), channel_id=1, source_target_pairs={{0,4},{4,0},{8,12},{12,8},{1,5},{5,1},{9,13},{13,9},{2,6},{6,2},{1... | collective-permute-start | bytes 786440 | tf_op jit(solution)/shard_map/ppermute | solution.py:86
  71.2 2.6 %collective-permute-start.5 = (bf16[1,8,128,128]{3,2,1,0:T(8,128)(2,1)S(1)}, bf16[1,8,128,128]{3,2,1,0:T(8,128)(2,1)S(1)}, u32[]{:S(2)}, u32[]{:S(2)}) collective-permute-start(bf16[1,8,128,128]{3,2,1,0:T(8,128)(2,1)S(1)} %get-tuple-element.13), channel_id=1, source_target_pairs={{0,8},{4,12},{8,0},{12,4},{1,9},{5,13},{9,1},{13,5},{2,10},{6,14},... | collective-permute-start | bytes 786440 | tf_op jit(solution)/shard_map/ppermute | solution.py:86
  73.8 0.0 collective-permute-start.6
  73.8 0.0 copy-done.8
  73.8 9.5 %collective-permute-done.4 = bf16[1,8,128,128]{3,2,1,0:T(8,128)(2,1)S(1)} collective-permute-done((bf16[1,8,128,128]{3,2,1,0:T(8,128)(2,1)S(1)}, bf16[1,8,128,128]{3,2,1,0:T(8,128)(2,1)S(1)}, u32[]{:S(2)}, u32[]{:S(2)}) %collective-permute-start.4) | collective-permute-done | bytes 262176 | tf_op jit(solution)/shard_map/ppermute | solution.py:86
  83.4 9.2 %collective-permute-done.5 = bf16[1,8,128,128]{3,2,1,0:T(8,128)(2,1)S(1)} collective-permute-done((bf16[1,8,128,128]{3,2,1,0:T(8,128)(2,1)S(1)}, bf16[1,8,128,128]{3,2,1,0:T(8,128)(2,1)S(1)}, u32[]{:S(2)}, u32[]{:S(2)}) %collective-permute-start.5) | collective-permute-done | bytes 262176 | tf_op jit(solution)/shard_map/ppermute | solution.py:86
  92.6 0.0 collective-permute-done.6
  92.6 0.0 copy-start.3
  92.6 0.3 convert_reduce_fusion
  93.0 1.3 fusion.20
  94.3 1.2 fusion.23
  95.6 0.0 copy-done.3
  95.6 1.0 convert_bitcast_fusion
  96.6 1.3 fusion.82
  97.9 6.8 %copy.23 = bf16[4,1024,4,32]{3,0,1,2:T(4,128)(2,1)} copy(bf16[4,1024,4,32]{1,3,2,0:T(8,128)(2,1)} %bitcast.158) | data formatting | bytes 2097152 | tf_op jit(solution)/shard_map/squeeze | solution.py:38
  104.7 4.7 %copy.24 = bf16[4,1024,4,32]{3,0,1,2:T(4,128)(2,1)} copy(bf16[4,1024,4,32]{1,3,2,0:T(8,128)(2,1)S(1)} %bitcast.157) | data formatting | bytes 2097152 | tf_op jit(solution)/shard_map/squeeze | solution.py:38
  109.4 8.8 %fusion.86 = f32[4,1024,4,4]{3,2,1,0:T(4,128)} fusion(bf16[4,1024,4,32]{3,0,1,2:T(4,128)(2,1)} %copy.23, bf16[4,1024,4,32]{3,0,1,2:T(4,128)(2,1)} %copy.24), kind=kOutput, calls=%fused_computation.224 | convolution fusion | flops 4194304 | bytes 2359296 | tf_op jit(solution)/shard_map/mphd,nphd->hmnp/dot_general | solution.py:37
  118.2 6.8 %copy.25 = f32[4,1024,4,4]{1,2,3,0:T(4,128)S(1)} copy(f32[4,1024,4,4]{3,2,1,0:T(4,128)} %fusion.86) | data formatting | bytes 524288 | tf_op jit(solution)/shard_map/mphd,nphd->hmnp/dot_general | solution.py:37
  125.1 0.4 fusion.85
  125.4 0.1 divide_convert_fusion
  125.5 5.5 %copy.27 = bf16[4,4,4,1024]{2,1,0,3:T(4,128)(2,1)} copy(bf16[4,4,4,1024]{3,2,1,0:T(4,128)(2,1)S(1)} %divide_convert_fusion) | data formatting | bytes 262144 | tf_op jit(solution)/shard_map/convert_element_type | solution.py:42
  131.0 5.4 %copy.26 = bf16[4,1024,4,32]{3,0,2,1:T(4,128)(2,1)} copy(bf16[4,1024,4,32]{1,3,2,0:T(8,128)(2,1)S(1)} %bitcast.156) | data formatting | bytes 2097152 | tf_op jit(solution)/shard_map/squeeze | solution.py:44
  136.4 8.3 %fusion.9 = bf16[4,1024,4,32]{3,0,2,1:T(4,128)(2,1)} fusion(bf16[4,1024,4,32]{3,0,2,1:T(4,128)(2,1)} %copy.26, bf16[4,4,4,1024]{2,1,0,3:T(4,128)(2,1)} %copy.27), kind=kOutput, calls=%fused_computation.51 | convolution fusion | flops 4718592 | bytes 2228224 | tf_op jit(solution)/shard_map/hmnp,nphd->mphd/dot_general | solution.py:43
  144.7 5.5 %copy.28 = bf16[4,1024,4,32]{1,3,2,0:T(8,128)(2,1)S(1)} copy(bf16[4,1024,4,32]{3,0,2,1:T(4,128)(2,1)} %fusion.9) | data formatting | bytes 2097152 | tf_op jit(solution)/shard_map/convert_element_type | solution.py:45
  150.2 0.0 copy-done.4
  150.2 0.5 fusion.24
  150.7 33.9 %all_to_all.12 = bf16[4,8,128,128]{3,2,1,0:T(8,128)(2,1)S(1)} all-to-all(bf16[4,8,128,128]{3,2,1,0:T(8,128)(2,1)S(1)} %bitcast.155), channel_id=1, replica_groups=mesh['group'=2,'ens'=4,'row'=2,'col'=2] {'ens'}, dimensions={0} | all-to-all | bytes 2097152 | tf_op jit(solution)/shard_map/all_to_all | solution.py:95
  184.7 1.0 copy.47
  (13 shorter events, 0.2 us)
Async XLA Ops:
  0.0 63.4 %copy-start = (bf16[512,128]{1,0:T(8,128)(2,1)S(1)}, bf16[512,128]{1,0:T(8,128)(2,1)}, u32[]{:S(2)}) copy-start(bf16[512,128]{1,0:T(8,128)(2,1)} %param.13) | copy-start | bytes 393220
  1.0 10.6 %collective-permute-start.1 = (bf16[1,3,128,128]{3,2,1,0:T(8,128)(2,1)S(1)}, bf16[1,3,128,128]{3,2,1,0:T(8,128)(2,1)S(1)}, u32[]{:S(2)}, u32[]{:S(2)}) collective-permute-start(bf16[1,3,128,128]{3,2,1,0:T(8,128)(2,1)S(1)} %get-tuple-element.19), channel_id=1, source_target_pairs={{2,0},{3,1},{6,4},{7,5},{10,8},{11,9},{14,12},{15,13},{18,16},{19,... | collective-permute-start | bytes 294920 | tf_op jit(solution)/shard_map/ppermute | solution.py:18
  2.3 7.0 %collective-permute-start = (bf16[1,3,128,128]{3,2,1,0:T(8,128)(2,1)S(1)}, bf16[1,3,128,128]{3,2,1,0:T(8,128)(2,1)S(1)}, u32[]{:S(2)}, u32[]{:S(2)}) collective-permute-start(bf16[1,3,128,128]{3,2,1,0:T(8,128)(2,1)S(1)} %get-tuple-element.20), channel_id=1, source_target_pairs={{0,2},{1,3},{4,6},{5,7},{8,10},{9,11},{12,14},{13,15},{16,18},{17,... | collective-permute-start | bytes 294920 | tf_op jit(solution)/shard_map/ppermute | solution.py:17
  9.4 9.6 %copy-start.1 = (bf16[1,32,128,128]{3,2,1,0:T(8,128)(2,1)S(1)}, bf16[1,32,128,128]{3,2,1,0:T(8,128)(2,1)}, u32[]{:S(2)}) copy-start(bf16[1,32,128,128]{3,2,1,0:T(8,128)(2,1)} %param.9) | copy-start | bytes 3145732
  11.7 1.0 copy-start.2
  13.4 5.6 %collective-permute-start.2 = (bf16[1,38,3,128]{3,2,1,0:T(4,128)(2,1)}, bf16[1,38,3,128]{3,2,1,0:T(4,128)(2,1)S(1)}, u32[]{:S(2)}, u32[]{:S(2)}) collective-permute-start(bf16[1,38,3,128]{3,2,1,0:T(4,128)(2,1)} %get-tuple-element.10), channel_id=1, source_target_pairs={{0,1},{2,3},{4,5},{6,7},{8,9},{10,11},{12,13},{14,15},{16,17},{18,... | collective-permute-start | bytes 87560 | tf_op jit(solution)/shard_map/ppermute | solution.py:17
  14.8 4.3 %collective-permute-start.3 = (bf16[1,38,3,128]{3,2,1,0:T(4,128)(2,1)}, bf16[1,38,3,128]{3,2,1,0:T(4,128)(2,1)S(1)}, u32[]{:S(2)}, u32[]{:S(2)}) collective-permute-start(bf16[1,38,3,128]{3,2,1,0:T(4,128)(2,1)} %get-tuple-element.11), channel_id=1, source_target_pairs={{1,0},{3,2},{5,4},{7,6},{9,8},{11,10},{13,12},{15,14},{17,16},{19,... | collective-permute-start | bytes 87560 | tf_op jit(solution)/shard_map/ppermute | solution.py:18
  60.0 1.4 copy-start.6
  61.3 2.1 %copy-start.7 = (bf16[128,512]{1,0:T(8,128)(2,1)S(1)}, bf16[128,512]{1,0:T(8,128)(2,1)}, u32[]{:S(2)}) copy-start(bf16[128,512]{1,0:T(8,128)(2,1)} %param.12) | copy-start | bytes 393220
  63.4 4.3 %copy-start.5 = (f32[128]{0:T(128)S(1)}, f32[128]{0:T(128)}, u32[]{:S(2)}) copy-start(f32[128]{0:T(128)} %convert_element_type.202) | copy-start | bytes 1540
  68.1 5.7 %copy-start.8 = (bf16[128]{0:T(256)(128)(2,1)S(1)}, bf16[128]{0:T(256)(128)(2,1)}, u32[]{:S(2)}) copy-start(bf16[128]{0:T(256)(128)(2,1)} %param.15) | copy-start | bytes 772
  68.4 14.9 %collective-permute-start.4 = (bf16[1,8,128,128]{3,2,1,0:T(8,128)(2,1)S(1)}, bf16[1,8,128,128]{3,2,1,0:T(8,128)(2,1)S(1)}, u32[]{:S(2)}, u32[]{:S(2)}) collective-permute-start(bf16[1,8,128,128]{3,2,1,0:T(8,128)(2,1)S(1)} %get-tuple-element.14), channel_id=1, source_target_pairs={{0,4},{4,0},{8,12},{12,8},{1,5},{5,1},{9,13},{13,9},{2,6},{6,2},{1... | collective-permute-start | bytes 786440 | tf_op jit(solution)/shard_map/ppermute | solution.py:86
  71.2 21.4 %collective-permute-start.5 = (bf16[1,8,128,128]{3,2,1,0:T(8,128)(2,1)S(1)}, bf16[1,8,128,128]{3,2,1,0:T(8,128)(2,1)S(1)}, u32[]{:S(2)}, u32[]{:S(2)}) collective-permute-start(bf16[1,8,128,128]{3,2,1,0:T(8,128)(2,1)S(1)} %get-tuple-element.13), channel_id=1, source_target_pairs={{0,8},{4,12},{8,0},{12,4},{1,9},{5,13},{9,1},{13,5},{2,10},{6,14},... | collective-permute-start | bytes 786440 | tf_op jit(solution)/shard_map/ppermute | solution.py:86
  73.8 18.8 %collective-permute-start.6 = (bf16[1,8,128,128]{3,2,1,0:T(8,128)(2,1)S(1)}, bf16[1,8,128,128]{3,2,1,0:T(8,128)(2,1)S(1)}, u32[]{:S(2)}, u32[]{:S(2)}) collective-permute-start(bf16[1,8,128,128]{3,2,1,0:T(8,128)(2,1)S(1)} %get-tuple-element.12), channel_id=1, source_target_pairs={{0,12},{4,8},{8,4},{12,0},{1,13},{5,9},{9,5},{13,1},{2,14},{6,10},... | collective-permute-start | bytes 786440 | tf_op jit(solution)/shard_map/ppermute | solution.py:86
  92.6 3.0 %copy-start.3 = (bf16[3,128,128]{2,1,0:T(8,128)(2,1)S(1)}, bf16[3,128,128]{2,1,0:T(8,128)(2,1)}, u32[]{:S(2)}) copy-start(bf16[3,128,128]{2,1,0:T(8,128)(2,1)} %param.16) | copy-start | bytes 294916
  144.7 5.5 %copy-start.4 = (bf16[128,128]{1,0:T(8,128)(2,1)S(1)}, bf16[128,128]{1,0:T(8,128)(2,1)}, u32[]{:S(2)}) copy-start(bf16[128,128]{1,0:T(8,128)(2,1)} %param.17) | copy-start | bytes 98308
